TPU v7x, 512 devices: a whole 4x8x8 slice. The times are simulated.
512 devices in a mesh: obs: 16 (over y, core), chan: 32 (over x, z).
Axes of the slice: x: 4, y: 8, z: 8, core: 2. Of those that a mesh axis runs over, the one named last changes fastest.
Arguments:
- visibilities: bfloat16 [16, 64, 384, 2, 2, 256], P('obs', None, 'chan'), may hold values from -6 to 6
- weights: int32 [16, 64, 384, 2], P('obs', None, 'chan'), may hold values from 0 to 16
- coverage: int32 [16, 64], P('obs'), may hold values from 0 to 255, as said below
- owner_map: int32 [256], replicated, may hold values from 0 to 255, as said below
Outputs:
- delay_cube: float32 [256, 2, 2, 256, 384], P('obs', None, None, 'chan')
Inputs may be any that keep to these rules, and one draw needn't show every extreme that they name: `coverage`: each row lists 64 different tiles. Of one observation's tiles at most 6 are held by one owner, the owner o holding the tiles owner_map[o * 16] to owner_map[(o + 1) * 16 - 1]; in every observation some owner holds exactly 6 of them. `owner_map`: A permutation of the tile numbers.
All inputs are finite; a program needn't handle non-finite values.
Results may differ from a plain program's by a relative error of at most 0.0037.
Values may be sent and summed in bfloat16 or wider, within the bound.
A program may use at most 128 MiB of HBM per device.

v0:
```python
import math

import jax
import jax.numpy as jnp
from jax import lax
from jax.sharding import PartitionSpec as P

NCHAN = 384


harris_terms = (0.35875, 0.48829, 0.14128, 0.01168)


def delay_table(length):
    index = jnp.arange(length, dtype=jnp.int32)
    phase = index[:, None] * index[None, :] % length
    angle = 2.0 * math.pi / length * phase.astype(jnp.float32)
    base = 2.0 * math.pi / (length - 1) * index.astype(jnp.float32)
    taper = (
        harris_terms[0]
        - harris_terms[1] * jnp.cos(base)
        + harris_terms[2] * jnp.cos(2.0 * base)
        - harris_terms[3] * jnp.cos(3.0 * base)
    )
    column = (taper / math.sqrt(length))[:, None]
    cosine = column * jnp.cos(angle)
    sine = column * jnp.sin(angle)
    table = jnp.stack([jnp.stack([cosine, -sine], 1), jnp.stack([sine, cosine], 1)], 0)
    return table.astype(jnp.bfloat16)


def locate_tiles(coverage, owner_map, owners):
    tiles_total = owner_map.shape[0]
    matches = coverage[:, :, None] == owner_map[None, None, :]
    places = jnp.sum(jnp.where(matches, jnp.arange(tiles_total, dtype=jnp.int32), 0), axis=-1)
    per_owner = tiles_total // owners
    return (places // per_owner, places % per_owner)


def bucket_selections(destination_owner, capacity, owners):
    table_entries = destination_owner.shape[1]
    order = jnp.arange(table_entries, dtype=jnp.int32)
    earlier = (destination_owner[:, :, None] == destination_owner[:, None, :]) & (
        order[None, None, :] < order[None, :, None]
    )
    rank = jnp.sum(earlier.astype(jnp.int32), axis=-1)
    target = destination_owner * capacity + rank
    slot_ids = jnp.arange(owners * capacity, dtype=jnp.int32)
    return target[:, None, :] == slot_ids[None, :, None]


def owner_sums(rec_vis, rec_weight, rec_slot, per_owner):
    slot_ids = jnp.arange(per_owner, dtype=jnp.int32)
    hits = (rec_slot[None] == slot_ids[:, None, None, None]).astype(jnp.bfloat16)
    counted = hits[..., None, None] * rec_weight[None]
    grid = jnp.einsum("jbsqcp,bsqcpxl->jcpxl", counted, rec_vis, preferred_element_type=jnp.float32)
    total = jnp.sum(counted.astype(jnp.float32), axis=(1, 2, 3))
    return (grid / jnp.maximum(total, 1.0)[..., None, None]).astype(jnp.bfloat16)


def shards(visibilities, weights, coverage, owner_map):
    owners = lax.axis_size("obs")
    batch = visibilities.shape[0]
    capacity = 3 * coverage.shape[1] // (2 * owners)
    per_owner = owner_map.shape[0] // owners
    destination_owner, target_slot = locate_tiles(coverage, owner_map, owners)
    picks = bucket_selections(destination_owner, capacity, owners)
    selections_float = picks.astype(jnp.float32)
    sent_slot = jnp.sum(jnp.where(picks, target_slot[:, None, :] + 1, 0), axis=-1) - 1
    sent_slot = sent_slot.reshape(batch, owners, capacity)
    sent_vis = jnp.einsum(
        "ehn,enymag->ehymag",
        picks.astype(jnp.bfloat16),
        visibilities,
        preferred_element_type=jnp.bfloat16,
    )
    sent_vis = sent_vis.reshape((batch, owners, capacity) + visibilities.shape[2:])
    weight_float = weights.astype(jnp.float32)
    table = delay_table(NCHAN)
    sent_weight = jnp.einsum(
        "gdw,gwoa->gdoa", selections_float, weight_float, precision=lax.Precision.HIGHEST
    ).astype(jnp.bfloat16)
    sent_weight = sent_weight.reshape((batch, owners, capacity) + weights.shape[2:])
    rec_vis, rec_weight, rec_slot = (
        lax.all_to_all(sent_vis, "obs", split_axis=1, concat_axis=1, tiled=True),
        lax.all_to_all(sent_weight, "obs", split_axis=1, concat_axis=1, tiled=True),
        lax.all_to_all(sent_slot, "obs", split_axis=1, concat_axis=1, tiled=True),
    )
    normalized = owner_sums(rec_vis, rec_weight, rec_slot, per_owner)
    return jnp.einsum(
        "inpal,anbq->ipblq",
        lax.all_to_all(normalized, "chan", split_axis=4, concat_axis=1, tiled=True),
        table,
        preferred_element_type=jnp.float32,
    )


def solution(mesh):
    return jax.shard_map(
        shards,
        mesh=mesh,
        in_specs=(
            P("obs", None, "chan", None, None, None),
            P("obs", None, "chan", None),
            P("obs", None),
            P(),
        ),
        out_specs=P("obs", None, None, "chan", None),
        check_vma=False,
    )
```

profile of v0, /device:TPU:1, one launch (start us, length us, event | category | flops | bytes accessed | tf_op | source)
XLA Modules:
  0.0 146.4 jit_solution(18295852071141251966)
XLA Ops:
  0.0 0.9 select_reduce_fusion
  0.9 0.2 convert_reduce_fusion.1
  1.1 0.1 select_reduce_fusion.1
  1.2 0.7 sub.46
  1.9 10.1 %all-to-all-start.1 = ((s32[1,16,6]{2,0,1:T(1,128)}), s32[1,16,6]{2,0,1:T(1,128)S(1)}, u32[]{:S(2)}, u32[]{:S(2)}) async-start(s32[1,16,6]{2,0,1:T(1,128)} %bitcast.12), calls=%async_computation.1 | async-start | bytes 16384 | tf_op jit(solution)/shard_map/all_to_all | solution.py:87
  12.0 0.7 convert_bitcast_fusion
  12.7 0.2 convolution_convert_fusion
  12.9 0.8 copy.52
  13.7 5.4 %all-to-all-done.1 = s32[1,16,6]{2,0,1:T(1,128)S(1)} async-done(((s32[1,16,6]{2,0,1:T(1,128)}), s32[1,16,6]{2,0,1:T(1,128)S(1)}, u32[]{:S(2)}, u32[]{:S(2)}) %all-to-all-start.1) | async-done | bytes 416 | tf_op jit(solution)/shard_map/all_to_all | solution.py:87
  19.1 4.0 %all-to-all-start.2 = ((bf16[1,16,6,12,2]{3,4,2,0,1:T(2,128)(2,1)}), bf16[1,16,6,12,2]{3,4,2,0,1:T(2,128)(2,1)S(1)}, u32[]{:S(2)}, u32[]{:S(2)}) async-start(bf16[1,16,6,12,2]{3,4,2,0,1:T(2,128)(2,1)} %bitcast.17), calls=%async_computation.2 | async-start | bytes 98304 | tf_op jit(solution)/shard_map/all_to_all | solution.py:86
  23.0 2.2 %convolution_bitcast_fusion = bf16[1,16,6,12,2,2,256]{6,1,5,4,3,2,0:T(8,128)(2,1)S(1)} fusion(bf16[64,12,2,2,256]{4,3,2,1,0:T(2,128)(2,1)} %bitcast.67, s32[16,6]{0,1:T(8,128)S(1)} %multiply_add_fusion, s32[64]{0:T(128)S(1)} %multiply_add_fusion.1), kind=kOutput, calls=%fused_computation.3 | convolution fusion | flops 151001088 | bytes 3932800 | tf_op jit(solution)/shard_map/ehn,enymag->ehymag/dot_general | solution.py:71
  25.2 3.6 %copy.47 = bf16[1,16,6,12,2,2,256]{6,5,4,3,2,0,1:T(2,128)(2,1)} copy(bf16[1,16,6,12,2,2,256]{6,1,5,4,3,2,0:T(8,128)(2,1)S(1)} %convolution_bitcast_fusion) | data formatting | bytes 4718592 | tf_op jit(solution)/shard_map/ehn,enymag->ehymag/dot_general | solution.py:71
  28.8 1.7 %all-to-all-done.2 = bf16[1,16,6,12,2]{3,4,2,0,1:T(2,128)(2,1)S(1)} async-done(((bf16[1,16,6,12,2]{3,4,2,0,1:T(2,128)(2,1)}), bf16[1,16,6,12,2]{3,4,2,0,1:T(2,128)(2,1)S(1)}, u32[]{:S(2)}, u32[]{:S(2)}) %all-to-all-start.2) | async-done | bytes 4640 | tf_op jit(solution)/shard_map/all_to_all | solution.py:86
  30.5 5.5 %all-to-all-start = ((bf16[1,16,6,12,2,2,256]{6,5,4,3,2,0,1:T(2,128)(2,1)}), bf16[1,16,6,12,2,2,256]{6,5,4,3,2,0,1:T(2,128)(2,1)S(1)}, u32[]{:S(2)}, u32[]{:S(2)}) async-start(bf16[1,16,6,12,2,2,256]{6,5,4,3,2,0,1:T(2,128)(2,1)} %copy.47), calls=%async_computation | async-start | bytes 4718592 | tf_op jit(solution)/shard_map/all_to_all | solution.py:85
  36.1 0.1 copy.50
  36.2 0.1 copy.54
  36.3 0.2 convert_reduce_fusion
  36.5 53.9 %all-to-all-done = bf16[1,16,6,12,2,2,256]{6,5,4,3,2,0,1:T(2,128)(2,1)S(1)} async-done(((bf16[1,16,6,12,2,2,256]{6,5,4,3,2,0,1:T(2,128)(2,1)}), bf16[1,16,6,12,2,2,256]{6,5,4,3,2,0,1:T(2,128)(2,1)S(1)}, u32[]{:S(2)}, u32[]{:S(2)}) %all-to-all-start) | async-done | bytes 2359328 | tf_op jit(solution)/shard_map/all_to_all | solution.py:85
  90.4 1.4 fusion
  91.9 0.1 fusion.6
  92.0 2.7 %copy.56 = bf16[16,12,2,2,256]{0,3,2,1,4:T(2,128)(2,1)S(1)} copy(bf16[16,12,2,2,256]{4,0,2,1,3:T(8,128)(2,1)S(1)} %fusion.6) | data formatting | bytes 786432 | tf_op jit(solution)/shard_map/convert_element_type | solution.py:58
  94.7 4.0 %reshape.558 = bf16[32,2,3072]{2,1,0:T(2,128)(2,1)} reshape(bf16[256,12,2,2,16]{4,3,2,1,0:T(2,128)(2,1)S(1)} %bitcast.64) | data formatting | bytes 786432
  98.8 11.5 %all-to-all-start.3 = ((bf16[32,2,3072]{2,1,0:T(2,128)(2,1)}), bf16[32,2,3072]{2,1,0:T(2,128)(2,1)S(1)}, u32[]{:S(2)}, u32[]{:S(2)}) async-start(bf16[32,2,3072]{2,1,0:T(2,128)(2,1)} %reshape.558), calls=%async_computation.3 | async-start | bytes 786432 | tf_op jit(solution)/shard_map/all_to_all | solution.py:92
  110.3 0.1 subtract_multiply_fusion
  110.4 2.7 %negate_convert_fusion = (bf16[384,1,384]{2,0,1:T(8,128)(2,1)S(1)}, bf16[384,1,384]{2,0,1:T(8,128)(2,1)S(1)}, bf16[384,1,384]{2,0,1:T(8,128)(2,1)S(1)}) fusion(f32[384]{0:T(512)S(1)} %subtract_multiply_fusion), kind=kLoop, calls=%fused_computation.21 | loop fusion | flops 2211840 | bytes 886272 | tf_op jit(solution)/shard_map/convert.7
  113.0 1.2 maximum_bitcast_fusion.2
  114.2 7.6 %all-to-all-done.3 = bf16[32,2,3072]{2,1,0:T(2,128)(2,1)S(1)} async-done(((bf16[32,2,3072]{2,1,0:T(2,128)(2,1)}), bf16[32,2,3072]{2,1,0:T(2,128)(2,1)S(1)}, u32[]{:S(2)}, u32[]{:S(2)}) %all-to-all-start.3) | async-done | bytes 393248 | tf_op jit(solution)/shard_map/all_to_all | solution.py:92
  121.8 3.3 %reshape.559 = bf16[256,12,2,2,16]{4,3,2,1,0:T(2,128)(2,1)} reshape(bf16[32,2,3072]{2,1,0:T(2,128)(2,1)S(1)} %all-to-all-done.3) | data formatting | bytes 786432
  125.0 2.7 %copy.81 = bf16[16,12,2,2,256]{0,4,3,2,1:T(8,128)(2,1)S(1)} copy(bf16[16,12,2,2,256]{0,3,2,1,4:T(2,128)(2,1)} %bitcast.65) | data formatting | bytes 786432 | tf_op jit(solution)/shard_map/all_to_all | solution.py:92
  127.7 8.9 %copy.69 = bf16[16,32,12,2,2,8]{2,1,0,4,5,3:T(8,128)(2,1)} copy(bf16[16,32,12,2,2,8]{0,5,1,4,3,2:T(8,128)(2,1)S(1)} %bitcast.63) | data formatting | bytes 786432 | tf_op jit(solution)/shard_map/all_to_all | solution.py:92
  136.6 0.0 copy-start
  136.6 0.0 copy-start.1
  136.6 8.2 %reshape.554 = bf16[16,384,2,2,8,1]{1,0,3,4,2,5:T(8,128)(2,1)S(1)} reshape(bf16[16,32,12,2,2,8]{2,1,0,4,5,3:T(8,128)(2,1)} %copy.69) | data formatting | bytes 786432 | tf_op jit(solution)/shard_map/all_to_all | solution.py:92
  144.8 0.0 copy-done
  144.8 0.0 copy-done.1
  144.8 0.5 convolution_bitcast_fusion.1
  145.3 1.1 copy.60
  (6 shorter events, 0.1 us)
Async XLA Ops:
  1.9 17.2 %all-to-all-start.1 = ((s32[1,16,6]{2,0,1:T(1,128)}), s32[1,16,6]{2,0,1:T(1,128)S(1)}, u32[]{:S(2)}, u32[]{:S(2)}) async-start(s32[1,16,6]{2,0,1:T(1,128)} %bitcast.12), calls=%async_computation.1 | async-start | bytes 16384 | tf_op jit(solution)/shard_map/all_to_all | solution.py:87
  19.1 11.5 %all-to-all-start.2 = ((bf16[1,16,6,12,2]{3,4,2,0,1:T(2,128)(2,1)}), bf16[1,16,6,12,2]{3,4,2,0,1:T(2,128)(2,1)S(1)}, u32[]{:S(2)}, u32[]{:S(2)}) async-start(bf16[1,16,6,12,2]{3,4,2,0,1:T(2,128)(2,1)} %bitcast.17), calls=%async_computation.2 | async-start | bytes 98304 | tf_op jit(solution)/shard_map/all_to_all | solution.py:86
  30.5 59.9 %all-to-all-start = ((bf16[1,16,6,12,2,2,256]{6,5,4,3,2,0,1:T(2,128)(2,1)}), bf16[1,16,6,12,2,2,256]{6,5,4,3,2,0,1:T(2,128)(2,1)S(1)}, u32[]{:S(2)}, u32[]{:S(2)}) async-start(bf16[1,16,6,12,2,2,256]{6,5,4,3,2,0,1:T(2,128)(2,1)} %copy.47), calls=%async_computation | async-start | bytes 4718592 | tf_op jit(solution)/shard_map/all_to_all | solution.py:85
  98.8 23.0 %all-to-all-start.3 = ((bf16[32,2,3072]{2,1,0:T(2,128)(2,1)}), bf16[32,2,3072]{2,1,0:T(2,128)(2,1)S(1)}, u32[]{:S(2)}, u32[]{:S(2)}) async-start(bf16[32,2,3072]{2,1,0:T(2,128)(2,1)} %reshape.558), calls=%async_computation.3 | async-start | bytes 786432 | tf_op jit(solution)/shard_map/all_to_all | solution.py:92
  136.6 8.2 %copy-start = (bf16[1,384,2,384]{3,1,0,2:T(8,128)(2,1)S(1)}, bf16[1,384,2,384]{3,1,0,2:T(8,128)(2,1)}, u32[]{:S(2)}) copy-start(bf16[1,384,2,384]{3,1,0,2:T(8,128)(2,1)} %get-tuple-element.5) | copy-start | bytes 1769476
  136.6 8.2 %copy-start.1 = (bf16[1,384,2,384]{3,1,0,2:T(8,128)(2,1)S(1)}, bf16[1,384,2,384]{3,1,0,2:T(8,128)(2,1)}, u32[]{:S(2)}) copy-start(bf16[1,384,2,384]{3,1,0,2:T(8,128)(2,1)} %get-tuple-element.6) | copy-start | bytes 1769476
where the time goes:
time: 149 us; the launch traced here: 146 us
  waiting for transfers between devices  68.6 us (46%)
  local copies, waits for them, and re-layouts  36.1 us (24%)
  starting transfers between devices  31.1 us (21%)
  other arithmetic  6.14 us (4%)
  matrix products  4.34 us (3%)
    all_to_all x1, waiting for transfers between devices, shards(): lax.all_to_all(sent_vis, 'obs', split_axis=1, concat_axis=1, tiled=True)  53.9 us
    all_to_all x3, local copies, waits for them, and re-layouts, shards(): lax.all_to_all(normalized, 'chan', split_axis=4, concat_axis=1, tiled=True)  19.7 us
    all_to_all x1, starting transfers between devices, shards(): lax.all_to_all(normalized, 'chan', split_axis=4, concat_axis=1, tiled=True)  11.5 us
    all_to_all x1, starting transfers between devices, shards(): lax.all_to_all(sent_slot, 'obs', split_axis=1, concat_axis=1, tiled=True)  10.1 us
    all_to_all x1, waiting for transfers between devices, shards(): lax.all_to_all(normalized, 'chan', split_axis=4, concat_axis=1, tiled=True)  7.58 us
    unnamed x6, local copies, waits for them, and re-layouts  7.3 us
    all_to_all x1, starting transfers between devices, shards(): lax.all_to_all(sent_vis, 'obs', split_axis=1, concat_axis=1, tiled=True)  5.54 us
    all_to_all x1, waiting for transfers between devices, shards(): lax.all_to_all(sent_slot, 'obs', split_axis=1, concat_axis=1, tiled=True)  5.39 us
  transfers between devices with their start and end apart: 4, of which 4 were waited for; matrix products, arithmetic and copies ran while one was open for 8% of the time, Pallas kernels for 0%

commit v1 on v0

v1 whole, which is shorter than its diff:
```python
import functools
import math

import jax
import jax.numpy as jnp
import ml_dtypes
import numpy as np
from jax import lax
from jax.experimental import pallas as pl
from jax.experimental.pallas import tpu as pltpu
from jax.sharding import PartitionSpec as P

F32, BF16, I32 = jnp.float32, jnp.bfloat16, jnp.int32
MESH = pl.DeviceIdType.MESH

NCHAN = 384
OCC = 64
TPO = 16
HALF = 8
NX, NY, NZ = 4, 8, 8
NCH = NX * NZ
LOCAL = NCHAN // NCH
PARTS = 3
CPP = LOCAL // PARTS
ROWS = CPP * 8
RIGHT, LEFT = 0, 1


def hops(way, half):
    return 4 if way == half else 3


def delay_table():
    n = np.arange(NCHAN)
    angle = 2.0 * math.pi * (np.outer(n, n) % NCHAN) / NCHAN
    base = 2.0 * math.pi * n / (NCHAN - 1)
    taper = 0.35875 - 0.48829 * np.cos(base) + 0.14128 * np.cos(2 * base) - 0.01168 * np.cos(3 * base)
    column = (taper / math.sqrt(NCHAN))[:, None]
    cosine, sine = column * np.cos(angle), column * np.sin(angle)
    table = np.stack([np.stack([cosine, -sine], 1), np.stack([sine, cosine], 1)], 0)
    table = table.astype(np.float32).astype(ml_dtypes.bfloat16)
    table = table.reshape(2, NCH, PARTS, CPP, 2 * NCHAN).transpose(2, 1, 3, 0, 4)
    return table.reshape(PARTS, NCH * CPP * 2, 2 * NCHAN)


def swap(lo, hi, mask, shift, axis):
    size = lo.shape[axis]
    new_lo = jnp.where(mask, pltpu.roll(hi, shift, axis), lo)
    new_hi = jnp.where(mask, hi, pltpu.roll(lo, size - shift, axis))
    return new_lo, new_hi


def block_transpose(blocks, unit, axis):
    blocks = list(blocks)
    group = lax.broadcasted_iota(I32, blocks[0].shape, axis) // unit
    step = 1
    while step < len(blocks):
        mask = (group // step) % 2 == 1
        for i in range(len(blocks)):
            if (i // step) % 2 == 0:
                blocks[i], blocks[i + step] = swap(blocks[i], blocks[i + step], mask, unit * step, axis)
        step *= 2
    return blocks


def kernel(
    vis, rw, inv, inv_v, tab, out,
    v0, v1, rw1, inv1_v, inv1, scaled, wt, tsend, trecv, tloc, rinv, send, recv, norm, mixed, outbox, inbox, tabv,
    s_v0, s_tab, s_inv, s_sib_s, s_sib_r, s_small_s, s_small_r, s_tot_s, s_tot_r, s_ring_s, s_ring_r, s_a2a_s, s_a2a_r,
):
    ob = lax.axis_index("obs")
    ch = lax.axis_index("chan")
    y, core = ob // 2, ob % 2
    x, z = ch // NZ, ch % NZ
    sibling = (y * 2 + 1 - core, ch)
    beside = {RIGHT: (((y + 1) % NY) * 2 + core, ch), LEFT: (((y + NY - 1) % NY) * 2 + core, ch)}

    def peer(d):
        return ((x + d // NZ) % NX) * NZ + (z + d % NZ) % NZ

    barrier = pltpu.get_barrier_semaphore()
    for device in (sibling, beside[RIGHT], beside[LEFT]):
        pl.semaphore_signal(barrier, inc=1, device_id=device, device_id_type=MESH)

    def greet(d, carry):
        pl.semaphore_signal(barrier, inc=1, device_id=(ob, peer(d)), device_id_type=MESH)
        return carry

    lax.fori_loop(1, NCH, greet, 0)

    load = [pltpu.make_async_copy(vis.at[:, pl.ds(s * ROWS, ROWS), :], v0.at[s], s_v0.at[s]) for s in range(PARTS)]
    load_tab = pltpu.make_async_copy(tab, tabv, s_tab)
    for copy in load:
        copy.start()
    load_tab.start()
    pl.semaphore_wait(barrier, NCH + 2)

    def remote(src, dst, s_sem, r_sem, device):
        return pltpu.make_async_remote_copy(
            src_ref=src, dst_ref=dst, send_sem=s_sem, recv_sem=r_sem, device_id=device, device_id_type=MESH
        )

    swaps = [
        remote(vis.at[:, pl.ds(s * ROWS, ROWS), :], v1.at[s], s_sib_s.at[s], s_sib_r.at[s], sibling) for s in range(PARTS)
    ]
    swap_rw = remote(rw, rw1, s_small_s.at[0], s_small_r.at[0], sibling)
    swap_inv = remote(inv_v, inv1_v, s_small_s.at[1], s_small_r.at[1], sibling)
    swap_inv.start()
    swap_rw.start()
    for copy in swaps:
        copy.start()

    for s in range(PARTS):
        for o in range(2):
            scaled[s, o, OCC] = jnp.zeros((ROWS, 128), F32)
    rinv[...] = jnp.zeros((128, 128), F32)
    wt[0] = rw[...].T
    swap_inv.wait_recv()
    to_smem = pltpu.make_async_copy(inv1_v, inv1, s_inv)
    to_smem.start()
    swap_rw.wait_recv()
    wt[1] = rw1[...].T
    to_smem.wait()

    def scale(s):
        for o, (v, w) in enumerate(((v0, rw), (v1, rw1))):
            if o == 0:
                load[s].wait()
            else:
                swaps[s].wait_recv()

            def body(g, weights):
                for j in range(4):
                    column = jnp.broadcast_to(weights[:, j : j + 1], (ROWS, 128))
                    scaled[s, o, g * 4 + j] = v[s, g * 4 + j].astype(F32) * column
                return pltpu.roll(weights, 124, 1)

            lax.fori_loop(0, OCC // 4, body, w[pl.ds(s * ROWS, ROWS), :])

    def slots(owner_y, i):
        t = (owner_y * 2 + core) * TPO + i
        return inv[t // 128, t % 128], inv1[t // 128, t % 128]

    def local(s, owner_y, i):
        k0, k1 = slots(owner_y, i)
        return scaled[s, 0, k0] + scaled[s, 1, k1]

    def owner_of(way, h, n):
        away = n - h + 1
        return (y + away) % NY if way == RIGHT else (y + NY - away) % NY

    ring, totals = {}, {}

    def emit(s, way, half, h):
        n = hops(way, half)
        owner = owner_of(way, h, n)
        if h > 1:
            ring[s, way, half, h - 1].wait_recv()

        def body(g, carry):
            for j in range(4):
                i = g * 4 + j
                acc = local(s, owner, half * HALF + i)
                if h > 1:
                    acc = acc + recv[s, way, half, h - 2, i].astype(F32)
                send[s, way, half, h - 1, i] = acc.astype(BF16)
            return carry

        lax.fori_loop(0, HALF // 4, body, 0)
        copy = remote(
            send.at[s, way, half, h - 1], recv.at[s, way, half, h - 1],
            s_ring_s.at[s, way, half, h - 1], s_ring_r.at[s, way, half, h - 1], beside[way],
        )
        copy.start()
        ring[s, way, half, h] = copy

    def local_totals(owner):
        def body(i, carry):
            k0, k1 = slots(owner, i)
            tloc[pl.ds(i, 1), :] = wt[0, pl.ds(k0, 1), :] + wt[1, pl.ds(k1, 1), :]
            return carry

        lax.fori_loop(0, TPO, body, 0)
        return tloc[...]

    def emit_total(way, h):
        n = hops(way, 0)
        acc = local_totals(owner_of(way, h, n))
        if h > 1:
            totals[way, h - 1].wait_recv()
            acc = acc + trecv[way, h - 2].astype(F32)
        tsend[way, h - 1] = acc.astype(BF16)
        copy = remote(
            tsend.at[way, h - 1], trecv.at[way, h - 1], s_tot_s.at[way, h - 1], s_tot_r.at[way, h - 1], beside[way]
        )
        copy.start()
        totals[way, h] = copy

    def total_inverse():
        acc = local_totals(y)
        for way in (RIGHT, LEFT):
            n = hops(way, 0)
            totals[way, n].wait_recv()
            acc = acc + trecv[way, n - 1].astype(F32)
        rinv[0:TPO, :] = 1.0 / jnp.maximum(acc, 1.0)
        rinv[...] = rinv[...].T

    sends = []

    def finish(s):
        factor = rinv[pl.ds(s * ROWS, ROWS), :]
        for half in range(2):
            for way in (RIGHT, LEFT):
                ring[s, way, half, hops(way, half)].wait_recv()
            for j in range(HALF):
                i = half * HALF + j
                acc = local(s, y, i)
                for way in (RIGHT, LEFT):
                    acc = acc + recv[s, way, half, hops(way, half) - 1, j].astype(F32)
                norm[i] = acc * jnp.broadcast_to(factor[:, i : i + 1], (ROWS, 128))

        def lanes(c, carry):
            blocks = [norm[i, pl.ds(c * 8, 8), :] for i in range(TPO)]
            for g, block in enumerate(block_transpose(blocks, 8, 1)):
                mixed[g, c] = block
            return carry

        lax.fori_loop(0, CPP, lanes, 0)

        def sublanes(g, carry):
            parts = block_transpose([mixed[g, c] for c in range(CPP)], 2, 0)
            for lh in range(2):
                outbox[s, lh * 16 + g] = jnp.concatenate([parts[lh], parts[2 + lh]], 0).astype(BF16)
            return carry

        lax.fori_loop(0, 16, sublanes, 0)

        def post(d, carry):
            to = peer(d)
            remote(outbox.at[s, to], inbox.at[s, ch], s_a2a_s.at[s], s_a2a_r.at[s], (ob, to)).start()
            return carry

        lax.fori_loop(1, NCH, post, 0)
        inbox[s, ch] = outbox[s, ch]

    def all_of(box, s, sem):
        some = box.at[s, pl.ds(0, NCH - 1)]
        return pltpu.make_async_copy(some, some, sem)

    def transform(s):
        all_of(inbox, s, s_a2a_r.at[s]).wait()
        if s == 0:
            load_tab.wait()
        cells = inbox[s].astype(F32).reshape(NCH, 2, 8, 128)
        for p in range(2):
            left = cells[:, p].reshape(NCH * 8, 128).T.astype(BF16)
            product = jnp.dot(left, tabv[s], preferred_element_type=F32)
            for b in range(2):
                block = product[:, b * NCHAN : (b + 1) * NCHAN].reshape(TPO, 8, NCHAN)
                out[:, p, b] = block if s == 0 else out[:, p, b] + block

    for tick in range(PARTS + 4):
        if tick < PARTS:
            scale(tick)
        for h in range(1, 5):
            s = tick - h + 1
            if 0 <= s < PARTS:
                for half in range(2):
                    for way in (RIGHT, LEFT):
                        if h <= hops(way, half):
                            emit(s, way, half, h)
                if s == 0:
                    for way in (RIGHT, LEFT):
                        if h <= hops(way, 0):
                            emit_total(way, h)
        if tick == 4:
            total_inverse()
        if tick >= 4:
            finish(tick - 4)
        if tick >= 5:
            transform(tick - 5)
    transform(PARTS - 1)

    for copy in [*swaps, swap_rw, swap_inv, *ring.values(), *totals.values()]:
        copy.wait_send()
    for s in range(PARTS):
        all_of(outbox, s, s_a2a_s.at[s]).wait()


def shards(visibilities, weights, coverage, owner_map):
    vis = visibilities.reshape(OCC, LOCAL, 2, 2, 2, 128).transpose(0, 1, 2, 4, 3, 5).reshape(OCC, LOCAL * 8, 128)
    rw = jnp.repeat(weights[0].transpose(1, 2, 0).reshape(LOCAL * 2, OCC), 4, axis=0).astype(F32)
    rw = jnp.pad(rw, ((0, 128 - LOCAL * 8), (0, 128 - OCC)))
    same = owner_map[:, None] == coverage[0][None, :]
    inv = OCC + jnp.sum(jnp.where(same, jnp.arange(OCC, dtype=I32) - OCC, 0), axis=1).astype(I32)
    inv = inv.reshape(2, 128)
    table = jnp.asarray(delay_table())

    vmem, smem, anywhere = (pl.BlockSpec(memory_space=m) for m in (pltpu.VMEM, pltpu.SMEM, pl.ANY))
    dma = pltpu.SemaphoreType.DMA
    return pl.pallas_call(
        kernel,
        out_shape=jax.ShapeDtypeStruct((TPO, 2, 2, 8, NCHAN), F32),
        in_specs=[anywhere, vmem, smem, vmem, anywhere],
        out_specs=vmem,
        scratch_shapes=[
            pltpu.VMEM((PARTS, OCC, ROWS, 128), BF16),
            pltpu.VMEM((PARTS, OCC, ROWS, 128), BF16),
            pltpu.VMEM((128, 128), F32),
            pltpu.VMEM((2, 128), I32),
            pltpu.SMEM((2, 128), I32),
            pltpu.VMEM((PARTS, 2, OCC + 1, ROWS, 128), F32),
            pltpu.VMEM((2, 128, 128), F32),
            pltpu.VMEM((2, 4, TPO, 128), BF16),
            pltpu.VMEM((2, 4, TPO, 128), BF16),
            pltpu.VMEM((TPO, 128), F32),
            pltpu.VMEM((128, 128), F32),
            pltpu.VMEM((PARTS, 2, 2, 4, HALF, ROWS, 128), BF16),
            pltpu.VMEM((PARTS, 2, 2, 4, HALF, ROWS, 128), BF16),
            pltpu.VMEM((TPO, ROWS, 128), F32),
            pltpu.VMEM((16, CPP, 8, 128), F32),
            pltpu.VMEM((PARTS, NCH, 16, 128), BF16),
            pltpu.VMEM((PARTS, NCH, 16, 128), BF16),
            pltpu.VMEM(table.shape, BF16),
            dma((PARTS,)),
            dma,
            dma,
            dma((PARTS,)),
            dma((PARTS,)),
            dma((2,)),
            dma((2,)),
            dma((2, 4)),
            dma((2, 4)),
            dma((PARTS, 2, 2, 4)),
            dma((PARTS, 2, 2, 4)),
            dma((PARTS,)),
            dma((PARTS,)),
        ],
        compiler_params=pltpu.CompilerParams(
            collective_id=0, has_side_effects=True, vmem_limit_bytes=48 * 1024 * 1024
        ),
    )(vis, rw, inv, inv, table)


def solution(mesh):
    return jax.shard_map(
        shards,
        mesh=mesh,
        in_specs=(
            P("obs", None, "chan", None, None, None),
            P("obs", None, "chan", None),
            P("obs", None),
            P(),
        ),
        out_specs=P("obs", None, None, "chan", None),
        check_vma=False,
    )
```

time: 149 us -> 72.6 us (0.49); the launches traced: 146 us -> 72.3 us
  waiting for transfers between devices: 68.6 us -> 0 us
  Pallas kernels: 0 us -> 67.2 us
  local copies, waits for them, and re-layouts: 36.1 us -> 3.57 us
  starting transfers between devices: 31.1 us -> 0 us
  other arithmetic: 6.14 us -> 1.5 us
  matrix products: 4.34 us -> 0 us
    all_to_all x4 -> x0, waiting for transfers between devices: 68.6 us -> none  [the longest x1 53.9 us: shards(): lax.all_to_all(sent_vis, 'obs', split_axis=1, concat_axis=1, tiled=True)]
    pallas_call x0 -> x1, Pallas kernels: none -> 67.2 us  [shards(): pl.pallas_call(kernel, out_shape=jax.ShapeDtypeStruct((TPO, 2, 2, 8, NCHA...]
    all_to_all x4 -> x0, starting transfers between devices: 31.1 us -> none  [the longest x1 11.5 us: shards(): lax.all_to_all(normalized, 'chan', split_axis=4, concat_axis=1, tiled=True)]
    all_to_all x4 -> x0, local copies, waits for them, and re-layouts: 19.8 us -> none  [the longest x3 19.7 us: shards(): lax.all_to_all(normalized, 'chan', split_axis=4, concat_axis=1, tiled=True)]
    another operation x3 -> x0, other arithmetic: 4.52 us -> none
    dot_general x4 -> x0, matrix products: 4.34 us -> none  [the longest x1 2.23 us: shards(): jnp.einsum('ehn,enymag->ehymag', picks.astype(jnp.bfloat16), visibilities...]
    unnamed x6 -> x5, local copies, waits for them, and re-layouts: 7.3 us -> 3.56 us
    dot_general x1 -> x0, local copies, waits for them, and re-layouts: 3.55 us -> none  [shards(): jnp.einsum('ehn,enymag->ehymag', picks.astype(jnp.bfloat16), visibilities...]
  transfers between devices with their start and end apart: 4 -> 0, of which waited for: 4 -> 0; matrix products, arithmetic and copies ran while one was open for 8% -> 0% of each run, Pallas kernels for 0% -> 0%
where the time goes in v1:
time: 72.6 us; the launch traced here: 72.3 us
  Pallas kernels  67.2 us (93%)
  local copies, waits for them, and re-layouts  3.57 us (5%)
  other arithmetic  1.5 us (2%)
    pallas_call x1, Pallas kernels, shards(): pl.pallas_call(kernel, out_shape=jax.ShapeDtypeStruct((TPO, 2, 2, 8, NCHA...  67.2 us
    unnamed x5, local copies, waits for them, and re-layouts  3.56 us

profile of v1, /device:TPU:1, one launch (start us, length us, event | category | flops | bytes accessed | tf_op | source)
XLA Modules:
  0.0 72.3 jit_solution(13113707113640592613)
XLA Ops:
  0.0 0.8 %select_reduce_fusion = s32[256]{0:T(256)S(1)} fusion(s32[64]{0:T(128)S(1)} %iota_add_fusion, s32[256]{0:T(256)} %param.8, s32[64]{0:T(128)} %bitcast.17), kind=kLoop, calls=%fused_computation | loop fusion | flops 48896 | bytes 2560 | tf_op jit(solution)/shard_map/reduce_sum | solution.py:295
  0.8 0.7 convert_element_type.18
  1.5 0.0 copy-start
  1.5 1.4 %copy-done = bf16[1,64,12,2,2,256]{5,4,3,2,1,0:T(2,128)(2,1)S(1)} copy-done((bf16[1,64,12,2,2,256]{5,4,3,2,1,0:T(2,128)(2,1)S(1)}, bf16[1,64,12,2,2,256]{5,4,3,2,1,0:T(2,128)(2,1)}, u32[]{:S(2)}) %copy-start) | copy-done | bytes 1572888
  2.9 0.0 copy-start.1
  2.9 1.3 %copy-done.1 = bf16[3,256,768]{2,1,0:T(8,128)(2,1)S(1)} copy-done((bf16[3,256,768]{2,1,0:T(8,128)(2,1)S(1)}, bf16[3,256,768]{2,1,0:T(8,128)(2,1)}, u32[]{:S(2)}) %copy-start.1) | copy-done | bytes 1179672
  4.2 67.2 %shard_map.55 = f32[16,2,2,8,384]{4,3,2,1,0:T(8,128)S(1)} custom-call(bf16[64,96,128]{2,1,0:T(8,128)(2,1)S(1)} %bitcast.14, f32[128,128]{1,0:T(8,128)S(1)} %pad.4.rw, s32[2,128]{1,0:T(2,128)S(1)} %add_bitcast_fusion.inv.inv_v, s32[2,128]{1,0:T(2,128)S(1)} %add_bitcast_fusion.inv.inv_v, bf16[3,256,768]{2,1,0:T(8,128)(2,1)S(1)} %copy-done.1), custom_call_target="tpu_custom_call" | custom-call | tf_op jit(solution)/shard_map/pallas_call | solution.py:301
  71.4 0.9 %copy.9 = f32[16,2,2,8,384]{4,3,2,1,0:T(8,128)} copy(f32[16,2,2,8,384]{4,3,2,1,0:T(8,128)S(1)} %shard_map.55) | data formatting | bytes 1572864
  (4 shorter events, 0.0 us)
Async XLA Ops:
  1.5 1.4 %copy-start = (bf16[1,64,12,2,2,256]{5,4,3,2,1,0:T(2,128)(2,1)S(1)}, bf16[1,64,12,2,2,256]{5,4,3,2,1,0:T(2,128)(2,1)}, u32[]{:S(2)}) copy-start(bf16[1,64,12,2,2,256]{5,4,3,2,1,0:T(2,128)(2,1)} %param.5) | copy-start | bytes 4718596
  2.9 1.3 %copy-start.1 = (bf16[3,256,768]{2,1,0:T(8,128)(2,1)S(1)}, bf16[3,256,768]{2,1,0:T(8,128)(2,1)}, u32[]{:S(2)}) copy-start(bf16[3,256,768]{2,1,0:T(8,128)(2,1)} %constant.11.clone.tab) | copy-start | bytes 3538948

commit v2 on v1

--- a/solution.py
+++ b/solution.py
@@ -40,7 +40,8 @@
     table = np.stack([np.stack([cosine, -sine], 1), np.stack([sine, cosine], 1)], 0)
     table = table.astype(np.float32).astype(ml_dtypes.bfloat16)
     table = table.reshape(2, NCH, PARTS, CPP, 2 * NCHAN).transpose(2, 1, 3, 0, 4)
-    return table.reshape(PARTS, NCH * CPP * 2, 2 * NCHAN)
+    table = table.reshape(PARTS, NCH * CPP * 2, 2 * NCHAN // 128, 128)
+    return table.transpose(0, 2, 1, 3)
 
 
 def swap(lo, hi, mask, shift, axis):
@@ -64,8 +65,8 @@
 
 
 def kernel(
-    vis, rw, inv, inv_v, tab, out,
-    v0, v1, rw1, inv1_v, inv1, scaled, wt, tsend, trecv, tloc, rinv, send, recv, norm, mixed, outbox, inbox, tabv,
+    vis, weights, coverage, owner_map, tab, out,
+    v0, v1, rw, rolled, slot_v, slot, tile_totals, scaled, tsend, trecv, rinv, send, recv, norm, mixed, outbox, inbox, tabv,
     s_v0, s_tab, s_inv, s_sib_s, s_sib_r, s_small_s, s_small_r, s_tot_s, s_tot_r, s_ring_s, s_ring_r, s_a2a_s, s_a2a_r,
 ):
     ob = lax.axis_index("obs")
@@ -93,6 +94,30 @@
     for copy in load:
         copy.start()
     load_tab.start()
+
+    rw[0] = jnp.zeros((128, 128), F32)
+    first = lax.broadcasted_iota(I32, (8, OCC), 0) < 4
+    for c in range(LOCAL):
+        pair = weights[c].astype(F32)
+        rw[0, c * 8 : (c + 1) * 8, 0:OCC] = jnp.where(first, pair[0:1], pair[1:2])
+    rinv[...] = jnp.zeros((128, 128), F32)
+    rinv[:, 0:OCC] = jnp.broadcast_to(coverage[...].astype(F32), (128, OCC))
+    listed = rinv[...].T
+    k = lax.broadcasted_iota(I32, (128, 128), 0)
+    for part in range(2):
+        same = (listed == owner_map[part : part + 1, :].astype(F32)) & (k < OCC)
+        slot_v[0, part : part + 1, :] = jnp.min(jnp.where(same, k, OCC), axis=0, keepdims=True)
+        totals_t = jnp.dot(rw[0].astype(BF16), same.astype(F32).astype(BF16), preferred_element_type=F32)
+        tile_totals[0, pl.ds(part * 128, 128), :] = totals_t.T
+
+    def roll_weights(o):
+        for g in range(4):
+            rolled[o, g] = rw[o] if g == 0 else pltpu.roll(rw[o], 128 - 16 * g, 1)
+
+    roll_weights(0)
+    for s in range(PARTS):
+        for o in range(2):
+            scaled[s, o, OCC] = jnp.zeros((ROWS, 128), F32)
     pl.semaphore_wait(barrier, NCH + 2)
 
     def remote(src, dst, s_sem, r_sem, device):
@@ -103,43 +128,34 @@
     swaps = [
         remote(vis.at[:, pl.ds(s * ROWS, ROWS), :], v1.at[s], s_sib_s.at[s], s_sib_r.at[s], sibling) for s in range(PARTS)
     ]
-    swap_rw = remote(rw, rw1, s_small_s.at[0], s_small_r.at[0], sibling)
-    swap_inv = remote(inv_v, inv1_v, s_small_s.at[1], s_small_r.at[1], sibling)
-    swap_inv.start()
-    swap_rw.start()
-    for copy in swaps:
+    smalls = [
+        remote(box.at[0], box.at[1], s_small_s.at[i], s_small_r.at[i], sibling)
+        for i, box in enumerate((slot_v, rw, tile_totals))
+    ]
+    smalls[0].start()
+    smalls[1].start()
+    swaps[0].start()
+    smalls[2].start()
+    for copy in swaps[1:]:
         copy.start()
-
-    for s in range(PARTS):
-        for o in range(2):
-            scaled[s, o, OCC] = jnp.zeros((ROWS, 128), F32)
-    rinv[...] = jnp.zeros((128, 128), F32)
-    wt[0] = rw[...].T
-    swap_inv.wait_recv()
-    to_smem = pltpu.make_async_copy(inv1_v, inv1, s_inv)
-    to_smem.start()
-    swap_rw.wait_recv()
-    wt[1] = rw1[...].T
-    to_smem.wait()
-
-    def scale(s):
-        for o, (v, w) in enumerate(((v0, rw), (v1, rw1))):
-            if o == 0:
-                load[s].wait()
-            else:
-                swaps[s].wait_recv()
-
-            def body(g, weights):
-                for j in range(4):
-                    column = jnp.broadcast_to(weights[:, j : j + 1], (ROWS, 128))
-                    scaled[s, o, g * 4 + j] = v[s, g * 4 + j].astype(F32) * column
-                return pltpu.roll(weights, 124, 1)
-
-            lax.fori_loop(0, OCC // 4, body, w[pl.ds(s * ROWS, ROWS), :])
+    to_smem = [pltpu.make_async_copy(slot_v.at[o], slot.at[o], s_inv.at[o]) for o in range(2)]
+    to_smem[0].start()
+
+    def scale(s, o):
+        v = (v0, v1)[o]
+
+        def body(g, carry):
+            columns = rolled[o, g, pl.ds(s * ROWS, ROWS), :]
+            for j in range(16):
+                column = jnp.broadcast_to(columns[:, j : j + 1], (ROWS, 128))
+                scaled[s, o, g * 16 + j] = v[s, g * 16 + j].astype(F32) * column
+            return carry
+
+        lax.fori_loop(0, OCC // 16, body, 0)
 
     def slots(owner_y, i):
         t = (owner_y * 2 + core) * TPO + i
-        return inv[t // 128, t % 128], inv1[t // 128, t % 128]
+        return slot[0, t // 128, t % 128], slot[1, t // 128, t % 128]
 
     def local(s, owner_y, i):
         k0, k1 = slots(owner_y, i)
@@ -175,13 +191,8 @@
         ring[s, way, half, h] = copy
 
     def local_totals(owner):
-        def body(i, carry):
-            k0, k1 = slots(owner, i)
-            tloc[pl.ds(i, 1), :] = wt[0, pl.ds(k0, 1), :] + wt[1, pl.ds(k1, 1), :]
-            return carry
-
-        lax.fori_loop(0, TPO, body, 0)
-        return tloc[...]
+        rows = pl.ds(pl.multiple_of((owner * 2 + core) * TPO, TPO), TPO)
+        return tile_totals[0, rows, :] + tile_totals[1, rows, :]
 
     def emit_total(way, h):
         n = hops(way, 0)
@@ -219,21 +230,14 @@
                     acc = acc + recv[s, way, half, hops(way, half) - 1, j].astype(F32)
                 norm[i] = acc * jnp.broadcast_to(factor[:, i : i + 1], (ROWS, 128))
 
-        def lanes(c, carry):
-            blocks = [norm[i, pl.ds(c * 8, 8), :] for i in range(TPO)]
+        for c in range(CPP):
+            blocks = [norm[i, c * 8 : (c + 1) * 8, :] for i in range(TPO)]
             for g, block in enumerate(block_transpose(blocks, 8, 1)):
                 mixed[g, c] = block
-            return carry
-
-        lax.fori_loop(0, CPP, lanes, 0)
-
-        def sublanes(g, carry):
+        for g in range(16):
             parts = block_transpose([mixed[g, c] for c in range(CPP)], 2, 0)
             for lh in range(2):
                 outbox[s, lh * 16 + g] = jnp.concatenate([parts[lh], parts[2 + lh]], 0).astype(BF16)
-            return carry
-
-        lax.fori_loop(0, 16, sublanes, 0)
 
         def post(d, carry):
             to = peer(d)
@@ -254,14 +258,26 @@
         cells = inbox[s].astype(F32).reshape(NCH, 2, 8, 128)
         for p in range(2):
             left = cells[:, p].reshape(NCH * 8, 128).T.astype(BF16)
-            product = jnp.dot(left, tabv[s], preferred_element_type=F32)
             for b in range(2):
-                block = product[:, b * NCHAN : (b + 1) * NCHAN].reshape(TPO, 8, NCHAN)
+                right = jnp.concatenate([tabv[s, 3 * b + j] for j in range(3)], 1)
+                block = jnp.dot(left, right, preferred_element_type=F32).reshape(TPO, 8, NCHAN)
                 out[:, p, b] = block if s == 0 else out[:, p, b] + block
 
     for tick in range(PARTS + 4):
         if tick < PARTS:
-            scale(tick)
+            load[tick].wait()
+            scale(tick, 0)
+            if tick == 0:
+                smalls[0].wait_recv()
+                to_smem[1].start()
+                smalls[1].wait_recv()
+                roll_weights(1)
+                for copy in to_smem:
+                    copy.wait()
+            swaps[tick].wait_recv()
+            scale(tick, 1)
+            if tick == 0:
+                smalls[2].wait_recv()
         for h in range(1, 5):
             s = tick - h + 1
             if 0 <= s < PARTS:
@@ -281,7 +297,7 @@
             transform(tick - 5)
     transform(PARTS - 1)
 
-    for copy in [*swaps, swap_rw, swap_inv, *ring.values(), *totals.values()]:
+    for copy in [*swaps, *smalls, *ring.values(), *totals.values()]:
         copy.wait_send()
     for s in range(PARTS):
         all_of(outbox, s, s_a2a_s.at[s]).wait()
@@ -289,31 +305,28 @@
 
 def shards(visibilities, weights, coverage, owner_map):
     vis = visibilities.reshape(OCC, LOCAL, 2, 2, 2, 128).transpose(0, 1, 2, 4, 3, 5).reshape(OCC, LOCAL * 8, 128)
-    rw = jnp.repeat(weights[0].transpose(1, 2, 0).reshape(LOCAL * 2, OCC), 4, axis=0).astype(F32)
-    rw = jnp.pad(rw, ((0, 128 - LOCAL * 8), (0, 128 - OCC)))
-    same = owner_map[:, None] == coverage[0][None, :]
-    inv = OCC + jnp.sum(jnp.where(same, jnp.arange(OCC, dtype=I32) - OCC, 0), axis=1).astype(I32)
-    inv = inv.reshape(2, 128)
+    weights = weights[0].transpose(1, 2, 0)
+    owner_map = owner_map.reshape(2, 128)
     table = jnp.asarray(delay_table())
 
-    vmem, smem, anywhere = (pl.BlockSpec(memory_space=m) for m in (pltpu.VMEM, pltpu.SMEM, pl.ANY))
+    vmem, hbm = (pl.BlockSpec(memory_space=m) for m in (pltpu.VMEM, pltpu.HBM))
     dma = pltpu.SemaphoreType.DMA
     return pl.pallas_call(
         kernel,
         out_shape=jax.ShapeDtypeStruct((TPO, 2, 2, 8, NCHAN), F32),
-        in_specs=[anywhere, vmem, smem, vmem, anywhere],
+        in_specs=[hbm, vmem, vmem, vmem, hbm],
         out_specs=vmem,
         scratch_shapes=[
             pltpu.VMEM((PARTS, OCC, ROWS, 128), BF16),
             pltpu.VMEM((PARTS, OCC, ROWS, 128), BF16),
-            pltpu.VMEM((128, 128), F32),
-            pltpu.VMEM((2, 128), I32),
-            pltpu.SMEM((2, 128), I32),
+            pltpu.VMEM((2, 128, 128), F32),
+            pltpu.VMEM((2, 4, 128, 128), F32),
+            pltpu.VMEM((2, 2, 128), I32),
+            pltpu.SMEM((2, 2, 128), I32),
+            pltpu.VMEM((2, 2 * 128, 128), F32),
             pltpu.VMEM((PARTS, 2, OCC + 1, ROWS, 128), F32),
-            pltpu.VMEM((2, 128, 128), F32),
             pltpu.VMEM((2, 4, TPO, 128), BF16),
             pltpu.VMEM((2, 4, TPO, 128), BF16),
-            pltpu.VMEM((TPO, 128), F32),
             pltpu.VMEM((128, 128), F32),
             pltpu.VMEM((PARTS, 2, 2, 4, HALF, ROWS, 128), BF16),
             pltpu.VMEM((PARTS, 2, 2, 4, HALF, ROWS, 128), BF16),
@@ -324,11 +337,11 @@
             pltpu.VMEM(table.shape, BF16),
             dma((PARTS,)),
             dma,
-            dma,
-            dma((PARTS,)),
-            dma((PARTS,)),
             dma((2,)),
-            dma((2,)),
+            dma((PARTS,)),
+            dma((PARTS,)),
+            dma((3,)),
+            dma((3,)),
             dma((2, 4)),
             dma((2, 4)),
             dma((PARTS, 2, 2, 4)),
@@ -337,9 +350,9 @@
             dma((PARTS,)),
         ],
         compiler_params=pltpu.CompilerParams(
-            collective_id=0, has_side_effects=True, vmem_limit_bytes=48 * 1024 * 1024
+            collective_id=0, has_side_effects=True, vmem_limit_bytes=62 * 1024 * 1024
         ),
-    )(vis, rw, inv, inv, table)
+    )(vis, weights, coverage, owner_map, table)
 
 
 def solution(mesh):

time: 72.6 us -> 66.8 us (0.920)
  Pallas kernels: 67.2 us -> 64.6 us
  other arithmetic: 1.5 us -> 0 us
  local copies, waits for them, and re-layouts: 3.57 us -> 2.07 us
    pallas_call x1, Pallas kernels: 67.2 us -> 64.6 us  [shards(): pl.pallas_call(kernel, out_shape=jax.ShapeDtypeStruct((TPO, 2, 2, 8, NCHA...]
    unnamed x5 -> x1, local copies, waits for them, and re-layouts: 3.56 us -> 2.07 us
    reduce_sum x1 -> x0, other arithmetic: 0.77 us -> none  [shards(): jnp.sum(jnp.where(same, jnp.arange(OCC, dtype=I32) - OCC, 0), axis=1)]
where the time goes in v2:
time: 66.8 us; the launch traced here: 66.6 us
  Pallas kernels  64.6 us (97%)
  local copies, waits for them, and re-layouts  2.07 us (3%)
    pallas_call x1, Pallas kernels, shards(): pl.pallas_call(kernel, out_shape=jax.ShapeDtypeStruct((TPO, 2, 2, 8, NCHA...  64.6 us
    unnamed x1, local copies, waits for them, and re-layouts  2.07 us

profile of v2, /device:TPU:1, one launch (start us, length us, event | category | flops | bytes accessed | tf_op | source)
XLA Modules:
  0.0 66.6 jit_solution(15147402521098933207)
XLA Ops:
  0.0 64.6 %shard_map.55 = f32[16,2,2,8,384]{4,3,2,1,0:T(8,128)} custom-call(bf16[64,96,128]{2,1,0:T(8,128)(2,1)} %bitcast.9, s32[12,2,64]{2,1,0:T(2,128)} %bitcast.10, s32[1,64]{1,0:T(1,128)} %coverage.1, s32[2,128]{1,0:T(2,128)} %bitcast.11, bf16[3,6,256,128]{3,2,1,0:T(8,128)(2,1)} %constant.2.clone.tab), custom_call_target="tpu_custom_call" | custom-call | tf_op jit(solution)/shard_map/pallas_call | solution.py:314
  64.6 2.1 %copy.8 = f32[16,2,2,8,384]{4,3,2,1,0:T(8,128)} copy(f32[16,2,2,8,384]{4,3,2,1,0:T(8,128)} %shard_map.55) | data formatting | bytes 1572864

commit v3 on v2

v3 whole, which is shorter than its diff:
```python
import functools
import math

import jax
import jax.numpy as jnp
import ml_dtypes
import numpy as np
from jax import lax
from jax.experimental import pallas as pl
from jax.experimental.pallas import tpu as pltpu
from jax.sharding import PartitionSpec as P

F32, BF16, I32 = jnp.float32, jnp.bfloat16, jnp.int32
MESH = pl.DeviceIdType.MESH

NCHAN = 384
OCC = 64
TPO = 16
CAP = 6
NX, NY, NZ = 4, 8, 8
NCH = NX * NZ
LOCAL = NCHAN // NCH
PARTS = 6
ROWS = LOCAL * 8 // PARTS
GROUPS = 3
CPG = LOCAL // GROUPS
LONG, SHORT = 0, 1
FIRST, SECOND, HOP, LAST = 0.0, 0.0, 2.0, 2.0
SLOT, SLOT1, ENTRY, RANKS, LISTS, RANK = 0, 1, 2, 3, 7, 7


def hops(chain):
    return 4 if chain == LONG else 3


def delay_table():
    n = np.arange(NCHAN)
    angle = 2.0 * math.pi * (np.outer(n, n) % NCHAN) / NCHAN
    base = 2.0 * math.pi * n / (NCHAN - 1)
    taper = 0.35875 - 0.48829 * np.cos(base) + 0.14128 * np.cos(2 * base) - 0.01168 * np.cos(3 * base)
    column = (taper / math.sqrt(NCHAN))[:, None]
    cosine, sine = column * np.cos(angle), column * np.sin(angle)
    table = np.stack([np.stack([cosine, -sine], 1), np.stack([sine, cosine], 1)], 0)
    table = table.astype(np.float32).astype(ml_dtypes.bfloat16)
    table = table.reshape(2, NCH, GROUPS, CPG, 2 * NCHAN).transpose(2, 1, 3, 0, 4)
    table = table.reshape(GROUPS, NCH * CPG * 2, 2 * NCHAN // 128, 128)
    return table.transpose(0, 2, 1, 3)


def swap(lo, hi, mask, shift, axis):
    size = lo.shape[axis]
    new_lo = jnp.where(mask, pltpu.roll(hi, shift, axis), lo)
    new_hi = jnp.where(mask, hi, pltpu.roll(lo, size - shift, axis))
    return new_lo, new_hi


def block_transpose(blocks, unit, axis):
    blocks = list(blocks)
    group = lax.broadcasted_iota(I32, blocks[0].shape, axis) // unit
    step = 1
    while step < len(blocks):
        mask = (group // step) % 2 == 1
        for i in range(len(blocks)):
            if (i // step) % 2 == 0:
                blocks[i], blocks[i + step] = swap(blocks[i], blocks[i + step], mask, unit * step, axis)
        step *= 2
    return blocks


def kernel(
    vis, weights, coverage, owner_map, tab, out,
    v0, v1, rw, counts, count_at, lists, listed_at, tile_totals, scaled, square, rinv, send1, recv1, got, send, recv, tsend, trecv,
    norm, mixed, outbox, inbox, tabv,
    s_v0, s_tab, s_counts, s_lists, s_sib_s, s_sib_r, s_small_s, s_small_r, s_rank_s, s_rank_r,
    s_one_s, s_one_r, s_ring_s, s_ring_r, s_tot_s, s_tot_r, s_a2a_s, s_a2a_r,
):
    ob = lax.axis_index("obs")
    ch = lax.axis_index("chan")
    y, core = ob // 2, ob % 2
    x, z = ch // NZ, ch % NZ
    sibling = (y * 2 + 1 - core, ch)
    above, below = (y + 1) % NY, (y + NY - 1) % NY

    def along(chain, parity, distance):
        sign = 1 - 2 * parity if chain == LONG else 2 * parity - 1
        return (y + NY + distance * sign) % NY

    def peer(d):
        return ((x + d // NZ) % NX) * NZ + (z + d % NZ) % NZ

    barrier = pltpu.get_barrier_semaphore()
    for device in [(near * 2 + c, ch) for near in (above, below) for c in range(2)] + [sibling]:
        pl.semaphore_signal(barrier, inc=1, device_id=device, device_id_type=MESH)

    def greet(d, carry):
        pl.semaphore_signal(barrier, inc=1, device_id=(ob, peer(d)), device_id_type=MESH)
        return carry

    lax.fori_loop(1, NCH, greet, 0)

    def part_of(ref, s):
        return ref.at[:, pl.ds(s * ROWS, ROWS), :]

    load = [pltpu.make_async_copy(part_of(vis, s), v0.at[s], s_v0.at[s]) for s in range(PARTS)]
    load_tab = pltpu.make_async_copy(tab, tabv, s_tab)
    for copy in load:
        copy.start()
    load_tab.start()

    rw[...] = jnp.zeros((128, 128), F32)
    first = lax.broadcasted_iota(I32, (8, OCC), 0) < 4
    for c in range(LOCAL):
        pair = weights[c].astype(F32)
        counts[0, c, :, 0:OCC] = pair
        rw[c * 8 : (c + 1) * 8, 0:OCC] = jnp.where(first, pair[0:1], pair[1:2])

    to_scalars = [pltpu.make_async_copy(counts.at[o], count_at.at[o], s_counts.at[o]) for o in range(2)]
    to_scalars[0].start()

    square[...] = jnp.zeros((128, 128), F32)
    square[:, 0:OCC] = jnp.broadcast_to(coverage[...].astype(F32), (128, OCC))
    number = square[...].T
    k = lax.broadcasted_iota(I32, (128, 128), 0)
    lane = lax.broadcasted_iota(I32, (128, 128), 1)
    same = [(number == owner_map[h : h + 1, :].astype(F32)) & (k < OCC) for h in range(2)]
    owner = sum(
        jnp.sum(jnp.where(same[h], ((lane + 128 * h) // TPO).astype(F32), 0.0), axis=1, keepdims=True) for h in range(2)
    )
    owner = jnp.broadcast_to(owner, (128, 128))
    earlier = (owner == owner.T) & (lane < k)
    rank = jnp.sum(jnp.where(earlier, 1.0, 0.0), axis=1, keepdims=True)
    rank = jnp.broadcast_to(jnp.minimum(rank, CAP * 1.0), (128, 128))
    for h in range(2):
        slot = jnp.min(jnp.where(same[h], k, OCC), axis=0, keepdims=True)
        before = (owner == ((lane + 128 * h) // TPO).astype(F32)) & (k < slot)
        count = jnp.minimum(jnp.sum(jnp.where(before, 1, 0), axis=0, keepdims=True), CAP)
        lists[SLOT, h : h + 1, :] = slot
        lists[RANK, h : h + 1, :] = jnp.where(slot < OCC, count, CAP)
    entry = owner * CAP + rank
    lists[ENTRY, 0:1, :] = jnp.min(
        jnp.where((entry == lane.astype(F32)) & (rank < CAP) & (k < OCC), k, OCC), axis=0, keepdims=True
    )
    lists[ENTRY, 1:2, :] = jnp.full((1, 128), OCC, I32)
    to_smem = [pltpu.make_async_copy(lists.at[i], listed_at.at[i], s_lists.at[i]) for i in range(LISTS)]
    to_smem[ENTRY].start()
    to_smem[SLOT].start()

    for s in range(PARTS):
        for o in range(2):
            scaled[s, o, OCC] = jnp.zeros((ROWS, 128), F32)
    for c in range(2):
        got[c, CAP] = jnp.zeros((ROWS, 128), F32)

    upper = lax.broadcasted_iota(I32, (8, 128), 0) < 4

    def scale(s, o):
        v = (v0, v1)[o]

        def body(g, carry):
            for j in range(8):
                k = g * 8 + j
                values = v[s, k].astype(F32)
                for c in range(2):
                    weight = jnp.where(upper, count_at[o, s * 2 + c, 0, k], count_at[o, s * 2 + c, 1, k])
                    scaled[s, o, k, c * 8 : c * 8 + 8] = values[c * 8 : c * 8 + 8] * weight
            return carry

        lax.fori_loop(0, OCC // 8, body, 0)

    def remote(src, dst, s_sem, r_sem, device):
        return pltpu.make_async_remote_copy(
            src_ref=src, dst_ref=dst, send_sem=s_sem, recv_sem=r_sem, device_id=device, device_id_type=MESH
        )

    sent = []

    def launch(copy):
        copy.start()
        sent.append(copy)
        return copy

    def arrived(ref, sem):
        pltpu.make_async_copy(ref, ref, sem).wait()

    def pack_first(s):
        for parity in range(2):
            for chain in (LONG, SHORT):
                base = (along(chain, parity, hops(chain)) * 2 + parity) * CAP
                for e in range(CAP):
                    send1[s, parity, chain, e] = scaled[s, 0, listed_at[ENTRY, 0, base + e]].astype(BF16)

    def send_first(s):
        for parity in range(2):
            for chain in (LONG, SHORT):
                launch(remote(
                    send1.at[s, parity, chain], recv1.at[s, chain, core],
                    s_one_s.at[s, parity, chain], s_one_r.at[s, chain, core],
                    (along(chain, parity, 1) * 2 + parity, ch),
                ))

    load[0].wait()
    to_scalars[0].wait()
    scale(0, 0)
    to_smem[ENTRY].wait()
    pack_first(0)

    for h in range(2):
        totals_t = jnp.dot(rw[...].astype(BF16), same[h].astype(F32).astype(BF16), preferred_element_type=F32)
        tile_totals[0, pl.ds(h * 128, 128), :] = totals_t.T

    pl.semaphore_wait(barrier, NCH + 4)

    smalls = [
        remote(src, dst, s_small_s.at[i], s_small_r.at[i], sibling)
        for i, (src, dst) in enumerate(
            ((lists.at[SLOT], lists.at[SLOT1]), (counts.at[0], counts.at[1]), (tile_totals.at[0], tile_totals.at[1]))
        )
    ]
    swaps = [remote(part_of(vis, s), v1.at[s], s_sib_s.at[s], s_sib_r.at[s], sibling) for s in range(PARTS)]
    send_first(0)
    launch(smalls[0])
    launch(smalls[1])
    launch(swaps[0])
    for side, near in ((0, above), (1, below)):
        for c in range(2):
            launch(remote(
                lists.at[RANK], lists.at[RANKS + side * 2 + core], s_rank_s.at[side, c], s_rank_r.at[side, core],
                (near * 2 + c, ch),
            ))
    launch(smalls[2])
    for copy in swaps[1:]:
        launch(copy)

    def local(s, tile):
        return scaled[s, 0, listed_at[SLOT, tile // 128, tile % 128]] + scaled[s, 1, listed_at[SLOT1, tile // 128, tile % 128]]

    ring, totals = {}, {}

    def emit(s, chain, h):
        owner_tiles = (along(chain, core, hops(chain) - h + 1) * 2 + core) * TPO
        if h > 2:
            ring[s, chain, h - 1].wait_recv()
        else:
            for c in range(2):
                arrived(recv1.at[s, chain, c], s_one_r.at[s, chain, c])
                got[c, 0:CAP] = recv1[s, chain, c].astype(F32)
        side = core if chain == LONG else 1 - core

        def body(g, carry):
            for j in range(8):
                i = g * 8 + j
                tile = owner_tiles + i
                acc = local(s, tile)
                if h > 2:
                    acc = acc + recv[s, chain, h - 3, i].astype(F32)
                else:
                    for c in range(2):
                        at = listed_at[RANKS + side * 2 + c, tile // 128, tile % 128]
                        acc = acc + got[c, at]
                send[s, chain, h - 2, i] = acc.astype(BF16)
            return carry

        lax.fori_loop(0, TPO // 8, body, 0)
        ring[s, chain, h] = launch(remote(
            send.at[s, chain, h - 2], recv.at[s, chain, h - 2],
            s_ring_s.at[s, chain, h - 2], s_ring_r.at[s, chain, h - 2], (along(chain, core, 1) * 2 + core, ch),
        ))

    def local_totals(owner_y):
        rows = pl.ds(pl.multiple_of((owner_y * 2 + core) * TPO, TPO), TPO)
        return tile_totals[0, rows, :] + tile_totals[1, rows, :]

    def emit_total(chain, h):
        acc = local_totals(along(chain, core, hops(chain) - h + 1))
        if h > 1:
            totals[chain, h - 1].wait_recv()
            acc = acc + trecv[chain, h - 2].astype(F32)
        tsend[chain, h - 1] = acc.astype(BF16)
        totals[chain, h] = launch(remote(
            tsend.at[chain, h - 1], trecv.at[chain, h - 1], s_tot_s.at[chain, h - 1], s_tot_r.at[chain, h - 1],
            (along(chain, core, 1) * 2 + core, ch),
        ))

    def total_inverse():
        acc = local_totals(y)
        for chain in (LONG, SHORT):
            totals[chain, hops(chain)].wait_recv()
            acc = acc + trecv[chain, hops(chain) - 1].astype(F32)
        square[0:TPO, :] = 1.0 / jnp.maximum(acc, 1.0)
        rinv[...] = square[...].T

    def settle(s):
        for chain in (LONG, SHORT):
            ring[s, chain, hops(chain)].wait_recv()
        factor = rinv[pl.ds(s * ROWS, ROWS), :]
        for i in range(TPO):
            acc = local(s, (y * 2 + core) * TPO + i)
            for chain in (LONG, SHORT):
                acc = acc + recv[s, chain, hops(chain) - 2, i].astype(F32)
            norm[i, s % 2] = acc * jnp.broadcast_to(factor[:, i : i + 1], (ROWS, 128))

    def exchange(g):
        for c in range(4):
            blocks = [norm[i, c // 2, (c % 2) * 8 : (c % 2) * 8 + 8, :] for i in range(TPO)]
            for group, block in enumerate(block_transpose(blocks, 8, 1)):
                mixed[group, c] = block
        for d in range(16):
            group = (ch + d) % 16
            parts = block_transpose([mixed[group, c] for c in range(4)], 2, 0)
            for lh in range(2):
                outbox[g, lh * 16 + group] = jnp.concatenate([parts[lh], parts[2 + lh]], 0).astype(BF16)
            for to in (group, 16 + group) if d else ((ch + 16) % NCH,):
                remote(outbox.at[g, to], inbox.at[g, ch], s_a2a_s.at[g], s_a2a_r.at[g], (ob, to)).start()
        inbox[g, ch] = outbox[g, ch]

    def transform(g):
        arrived(inbox.at[g, pl.ds(0, NCH - 1)], s_a2a_r.at[g])
        if g == 0:
            load_tab.wait()
        cells = inbox[g].astype(F32).reshape(NCH, 2, 8, 128)
        for p in range(2):
            left = cells[:, p].reshape(NCH * 8, 128).T.astype(BF16)
            for b in range(2):
                right = jnp.concatenate([tabv[g, 3 * b + j] for j in range(3)], 1)
                block = jnp.dot(left, right, preferred_element_type=F32).reshape(TPO, 8, NCHAN)
                out[:, p, b] = block if g == 0 else out[:, p, b] + block

    def first(s):
        if s:
            load[s].wait()
            scale(s, 0)
            pack_first(s)
            send_first(s)

    def second(s):
        if s == 0:
            smalls[0].wait_recv()
            to_smem[SLOT1].start()
            smalls[1].wait_recv()
            to_scalars[1].start()
            for side in range(2):
                for c in range(2):
                    arrived(lists.at[RANKS + side * 2 + c], s_rank_r.at[side, c])
                    to_smem[RANKS + side * 2 + c].start()
            for i in range(LISTS):
                if i != ENTRY:
                    to_smem[i].wait()
            to_scalars[1].wait()
        swaps[s].wait_recv()
        scale(s, 1)

    def hop(s, h):
        for chain in (LONG, SHORT):
            if h <= hops(chain):
                emit(s, chain, h)
        if s == 0:
            if h == 2:
                smalls[2].wait_recv()
                emit_total(LONG, 1)
                emit_total(SHORT, 1)
            for chain in (LONG, SHORT):
                if h <= hops(chain):
                    emit_total(chain, h)

    def last(s):
        if s == 0:
            total_inverse()
        settle(s)
        if s % 2:
            exchange(s // 2)

    steps = []
    for s in range(PARTS):
        steps.append((FIRST * s, 0, s, first, (s,)))
        steps.append((s + HOP - SECOND, 1, s, second, (s,)))
        for h in range(2, 5):
            steps.append((s + HOP * (h - 1), h, s, hop, (s, h)))
        steps.append((s + HOP * 3 + LAST, 5, s, last, (s,)))
    for *_, step, which in sorted(steps, key=lambda step: step[:3]):
        step(*which)
    for g in range(GROUPS):
        transform(g)

    for copy in sent:
        copy.wait_send()
    for g in range(GROUPS):
        arrived(outbox.at[g, pl.ds(0, NCH - 1)], s_a2a_s.at[g])


def shards(visibilities, weights, coverage, owner_map):
    vis = visibilities.reshape(OCC, LOCAL, 2, 2, 2, 128).transpose(0, 1, 2, 4, 3, 5).reshape(OCC, LOCAL * 8, 128)
    weights = weights[0].transpose(1, 2, 0)
    owner_map = owner_map.reshape(2, 128)
    table = jnp.asarray(delay_table())

    vmem, hbm = (pl.BlockSpec(memory_space=m) for m in (pltpu.VMEM, pltpu.HBM))
    dma = pltpu.SemaphoreType.DMA
    return pl.pallas_call(
        kernel,
        out_shape=jax.ShapeDtypeStruct((TPO, 2, 2, 8, NCHAN), F32),
        in_specs=[hbm, vmem, vmem, vmem, hbm],
        out_specs=vmem,
        scratch_shapes=[
            pltpu.VMEM((PARTS, OCC, ROWS, 128), BF16),
            pltpu.VMEM((PARTS, OCC, ROWS, 128), BF16),
            pltpu.VMEM((128, 128), F32),
            pltpu.VMEM((2, LOCAL, 2, 128), F32),
            pltpu.SMEM((2, LOCAL, 2, 128), F32),
            pltpu.VMEM((LISTS + 1, 2, 128), I32),
            pltpu.SMEM((LISTS, 2, 128), I32),
            pltpu.VMEM((2, 2 * 128, 128), F32),
            pltpu.VMEM((PARTS, 2, OCC + 1, ROWS, 128), F32),
            pltpu.VMEM((128, 128), F32),
            pltpu.VMEM((128, 128), F32),
            pltpu.VMEM((PARTS, 2, 2, CAP, ROWS, 128), BF16),
            pltpu.VMEM((PARTS, 2, 2, CAP, ROWS, 128), BF16),
            pltpu.VMEM((2, CAP + 1, ROWS, 128), F32),
            pltpu.VMEM((PARTS, 2, 3, TPO, ROWS, 128), BF16),
            pltpu.VMEM((PARTS, 2, 3, TPO, ROWS, 128), BF16),
            pltpu.VMEM((2, 4, TPO, 128), BF16),
            pltpu.VMEM((2, 4, TPO, 128), BF16),
            pltpu.VMEM((TPO, 2, ROWS, 128), F32),
            pltpu.VMEM((16, CPG, 8, 128), F32),
            pltpu.VMEM((GROUPS, NCH, 16, 128), BF16),
            pltpu.VMEM((GROUPS, NCH, 16, 128), BF16),
            pltpu.VMEM(table.shape, BF16),
            dma((PARTS,)),
            dma,
            dma((2,)),
            dma((LISTS,)),
            dma((PARTS,)),
            dma((PARTS,)),
            dma((3,)),
            dma((3,)),
            dma((2, 2)),
            dma((2, 2)),
            dma((PARTS, 2, 2)),
            dma((PARTS, 2, 2)),
            dma((PARTS, 2, 3)),
            dma((PARTS, 2, 3)),
            dma((2, 4)),
            dma((2, 4)),
            dma((GROUPS,)),
            dma((GROUPS,)),
        ],
        compiler_params=pltpu.CompilerParams(
            collective_id=0, has_side_effects=True, vmem_limit_bytes=60 * 1024 * 1024
        ),
    )(vis, weights, coverage, owner_map, table)


def solution(mesh):
    return jax.shard_map(
        shards,
        mesh=mesh,
        in_specs=(
            P("obs", None, "chan", None, None, None),
            P("obs", None, "chan", None),
            P("obs", None),
            P(),
        ),
        out_specs=P("obs", None, None, "chan", None),
        check_vma=False,
    )
```

time: 66.8 us -> 61.3 us (0.918); the launches traced: 66.6 us -> 60.5 us
  Pallas kernels: 64.6 us -> 58.4 us
    pallas_call x1, Pallas kernels: 64.6 us -> 58.4 us  [shards(): pl.pallas_call(kernel, out_shape=jax.ShapeDtypeStruct((TPO, 2, 2, 8, NCHA...]
where the time goes in v3:
time: 61.3 us; the launch traced here: 60.5 us
  Pallas kernels  58.4 us (95%)
  local copies, waits for them, and re-layouts  2.07 us (3%)
    pallas_call x1, Pallas kernels, shards(): pl.pallas_call(kernel, out_shape=jax.ShapeDtypeStruct((TPO, 2, 2, 8, NCHA...  58.4 us
    unnamed x1, local copies, waits for them, and re-layouts  2.07 us

profile of v3, /device:TPU:1, one launch (start us, length us, event | category | flops | bytes accessed | tf_op | source)
XLA Modules:
  0.0 60.5 jit_solution(3873828301142271396)
XLA Ops:
  0.0 58.4 %shard_map.55 = f32[16,2,2,8,384]{4,3,2,1,0:T(8,128)} custom-call(bf16[64,96,128]{2,1,0:T(8,128)(2,1)} %bitcast.9, s32[12,2,64]{2,1,0:T(2,128)} %bitcast.10, s32[1,64]{1,0:T(1,128)} %coverage.1, s32[2,128]{1,0:T(2,128)} %bitcast.11, bf16[3,6,256,128]{3,2,1,0:T(8,128)(2,1)} %constant.2.clone.tab), custom_call_target="tpu_custom_call" | custom-call | tf_op jit(solution)/shard_map/pallas_call | solution.py:398
  58.4 2.1 %copy.8 = f32[16,2,2,8,384]{4,3,2,1,0:T(8,128)} copy(f32[16,2,2,8,384]{4,3,2,1,0:T(8,128)} %shard_map.55) | data formatting | bytes 1572864

commit v4 on v3

--- a/solution.py
+++ b/solution.py
@@ -25,6 +25,7 @@
 GROUPS = 3
 CPG = LOCAL // GROUPS
 LONG, SHORT = 0, 1
+FAR_FIRST = (4, 12, 3, 11, 5, 13, 2, 10, 6, 14, 1, 9, 7, 15, 8, 0)
 FIRST, SECOND, HOP, LAST = 0.0, 0.0, 2.0, 2.0
 SLOT, SLOT1, ENTRY, RANKS, LISTS, RANK = 0, 1, 2, 3, 7, 7
 
@@ -304,7 +305,7 @@
             blocks = [norm[i, c // 2, (c % 2) * 8 : (c % 2) * 8 + 8, :] for i in range(TPO)]
             for group, block in enumerate(block_transpose(blocks, 8, 1)):
                 mixed[group, c] = block
-        for d in range(16):
+        for d in FAR_FIRST:
             group = (ch + d) % 16
             parts = block_transpose([mixed[group, c] for c in range(4)], 2, 0)
             for lh in range(2):
@@ -378,13 +379,13 @@
         steps.append((s + HOP * 3 + LAST, 5, s, last, (s,)))
     for *_, step, which in sorted(steps, key=lambda step: step[:3]):
         step(*which)
-    for g in range(GROUPS):
+    for g in range(GROUPS - 1):
         transform(g)
-
     for copy in sent:
         copy.wait_send()
     for g in range(GROUPS):
         arrived(outbox.at[g, pl.ds(0, NCH - 1)], s_a2a_s.at[g])
+    transform(GROUPS - 1)
 
 
 def shards(visibilities, weights, coverage, owner_map):
@@ -444,7 +445,7 @@
             dma((GROUPS,)),
         ],
         compiler_params=pltpu.CompilerParams(
-            collective_id=0, has_side_effects=True, vmem_limit_bytes=60 * 1024 * 1024
+            collective_id=0, has_side_effects=True, vmem_limit_bytes=53 * 1024 * 1024
         ),
     )(vis, weights, coverage, owner_map, table)
 

time: 61.3 us -> 60.1 us (0.980)
  Pallas kernels: 58.4 us -> 56.7 us
  local copies, waits for them, and re-layouts: 2.07 us -> 2.92 us
    pallas_call x1, Pallas kernels: 58.4 us -> 56.7 us  [shards(): pl.pallas_call(kernel, out_shape=jax.ShapeDtypeStruct((TPO, 2, 2, 8, NCHA...]
    unnamed x1 -> x7, local copies, waits for them, and re-layouts: 2.07 us -> 2.92 us
where the time goes in v4:
time: 60.1 us; the launch traced here: 59.6 us
  Pallas kernels  56.7 us (94%)
  local copies, waits for them, and re-layouts  2.92 us (5%)
    pallas_call x1, Pallas kernels, shards(): pl.pallas_call(kernel, out_shape=jax.ShapeDtypeStruct((TPO, 2, 2, 8, NCHA...  56.7 us
    unnamed x7, local copies, waits for them, and re-layouts  2.92 us

profile of v4, /device:TPU:1, one launch (start us, length us, event | category | flops | bytes accessed | tf_op | source)
XLA Modules:
  0.0 59.6 jit_solution(12359510623109303339)
XLA Ops:
  0.0 0.0 copy-start
  0.0 0.7 %copy-done = s32[1,64,12,2]{1,3,2,0:T(2,128)S(1)} copy-done((s32[1,64,12,2]{1,3,2,0:T(2,128)S(1)}, s32[1,64,12,2]{1,3,2,0:T(2,128)}, u32[]{:S(2)}) %copy-start) | copy-done | bytes 6168
  0.7 0.0 copy-start.1
  0.7 0.7 %copy-done.1 = s32[256]{0:T(256)S(1)} copy-done((s32[256]{0:T(256)S(1)}, s32[256]{0:T(256)}, u32[]{:S(2)}) %copy-start.1) | copy-done | bytes 1048
  1.4 0.0 copy-start.2
  1.4 0.7 %copy-done.2 = s32[1,64]{1,0:T(1,128)S(1)} copy-done((s32[1,64]{1,0:T(1,128)S(1)}, s32[1,64]{1,0:T(1,128)}, u32[]{:S(2)}) %copy-start.2) | copy-done | bytes 280
  2.0 56.7 %shard_map.55 = f32[16,2,2,8,384]{4,3,2,1,0:T(8,128)S(1)} custom-call(bf16[64,96,128]{2,1,0:T(8,128)(2,1)} %bitcast.11, s32[12,2,64]{2,1,0:T(2,128)S(1)} %bitcast.9, s32[1,64]{1,0:T(1,128)S(1)} %copy-done.2, s32[2,128]{1,0:T(2,128)S(1)} %bitcast.10, bf16[3,6,256,128]{3,2,1,0:T(8,128)(2,1)} %constant.2.clone.tab), custom_call_target="tpu_custom_call" | custom-call | tf_op jit(solution)/shard_map/pallas_call | solution.py:399
  58.8 0.9 %copy.8 = f32[16,2,2,8,384]{4,3,2,1,0:T(8,128)} copy(f32[16,2,2,8,384]{4,3,2,1,0:T(8,128)S(1)} %shard_map.55) | data formatting | bytes 1572864
Async XLA Ops:
  0.0 0.7 %copy-start = (s32[1,64,12,2]{1,3,2,0:T(2,128)S(1)}, s32[1,64,12,2]{1,3,2,0:T(2,128)}, u32[]{:S(2)}) copy-start(s32[1,64,12,2]{1,3,2,0:T(2,128)} %param.6) | copy-start | bytes 18436
  0.7 0.7 %copy-start.1 = (s32[256]{0:T(256)S(1)}, s32[256]{0:T(256)}, u32[]{:S(2)}) copy-start(s32[256]{0:T(256)} %param.8) | copy-start | bytes 3076
  1.4 0.7 %copy-start.2 = (s32[1,64]{1,0:T(1,128)S(1)}, s32[1,64]{1,0:T(1,128)}, u32[]{:S(2)}) copy-start(s32[1,64]{1,0:T(1,128)} %coverage.1) | copy-start | bytes 772

commit v5 on v4

--- a/solution.py
+++ b/solution.py
@@ -69,7 +69,7 @@
 
 
 def kernel(
-    vis, weights, coverage, owner_map, tab, out,
+    vis, small, tab, out,
     v0, v1, rw, counts, count_at, lists, listed_at, tile_totals, scaled, square, rinv, send1, recv1, got, send, recv, tsend, trecv,
     norm, mixed, outbox, inbox, tabv,
     s_v0, s_tab, s_counts, s_lists, s_sib_s, s_sib_r, s_small_s, s_small_r, s_rank_s, s_rank_r,
@@ -111,7 +111,7 @@
     rw[...] = jnp.zeros((128, 128), F32)
     first = lax.broadcasted_iota(I32, (8, OCC), 0) < 4
     for c in range(LOCAL):
-        pair = weights[c].astype(F32)
+        pair = small[2 * c : 2 * c + 2, 0:OCC].astype(F32)
         counts[0, c, :, 0:OCC] = pair
         rw[c * 8 : (c + 1) * 8, 0:OCC] = jnp.where(first, pair[0:1], pair[1:2])
 
@@ -119,11 +119,11 @@
     to_scalars[0].start()
 
     square[...] = jnp.zeros((128, 128), F32)
-    square[:, 0:OCC] = jnp.broadcast_to(coverage[...].astype(F32), (128, OCC))
+    square[:, 0:OCC] = jnp.broadcast_to(small[2 * LOCAL : 2 * LOCAL + 1, 0:OCC].astype(F32), (128, OCC))
     number = square[...].T
     k = lax.broadcasted_iota(I32, (128, 128), 0)
     lane = lax.broadcasted_iota(I32, (128, 128), 1)
-    same = [(number == owner_map[h : h + 1, :].astype(F32)) & (k < OCC) for h in range(2)]
+    same = [(number == small[2 * LOCAL + 1 + h : 2 * LOCAL + 2 + h, :].astype(F32)) & (k < OCC) for h in range(2)]
     owner = sum(
         jnp.sum(jnp.where(same[h], ((lane + 128 * h) // TPO).astype(F32), 0.0), axis=1, keepdims=True) for h in range(2)
     )
@@ -390,8 +390,9 @@
 
 def shards(visibilities, weights, coverage, owner_map):
     vis = visibilities.reshape(OCC, LOCAL, 2, 2, 2, 128).transpose(0, 1, 2, 4, 3, 5).reshape(OCC, LOCAL * 8, 128)
-    weights = weights[0].transpose(1, 2, 0)
-    owner_map = owner_map.reshape(2, 128)
+    weights = weights[0].transpose(1, 2, 0).reshape(2 * LOCAL, OCC)
+    small = jnp.pad(jnp.concatenate([weights, coverage], 0), ((0, 0), (0, 128 - OCC)))
+    small = jnp.concatenate([small, owner_map.reshape(2, 128)], 0)
     table = jnp.asarray(delay_table())
 
     vmem, hbm = (pl.BlockSpec(memory_space=m) for m in (pltpu.VMEM, pltpu.HBM))
@@ -399,7 +400,7 @@
     return pl.pallas_call(
         kernel,
         out_shape=jax.ShapeDtypeStruct((TPO, 2, 2, 8, NCHAN), F32),
-        in_specs=[hbm, vmem, vmem, vmem, hbm],
+        in_specs=[hbm, vmem, hbm],
         out_specs=vmem,
         scratch_shapes=[
             pltpu.VMEM((PARTS, OCC, ROWS, 128), BF16),
@@ -447,7 +448,7 @@
         compiler_params=pltpu.CompilerParams(
             collective_id=0, has_side_effects=True, vmem_limit_bytes=53 * 1024 * 1024
         ),
-    )(vis, weights, coverage, owner_map, table)
+    )(vis, small, table)
 
 
 def solution(mesh):

time: 60.1 us -> 59.5 us (0.990)
  local copies, waits for them, and re-layouts: 2.92 us -> 0.88 us
  other arithmetic: 0 us -> 1.41 us
    unnamed x7 -> x1, local copies, waits for them, and re-layouts: 2.92 us -> 0.88 us
    concatenate x0 -> x2, other arithmetic: none -> 1.41 us  [the longest x1 0.73 us: shards(): jnp.concatenate([weights, coverage], 0)]
where the time goes in v5:
time: 59.5 us; the launch traced here: 59 us
  Pallas kernels  56.7 us (95%)
  other arithmetic  1.41 us (2%)
  local copies, waits for them, and re-layouts  0.88 us (1%)
    pallas_call x1, Pallas kernels, shards(): pl.pallas_call(kernel, out_shape=jax.ShapeDtypeStruct((TPO, 2, 2, 8, NCHA...  56.7 us

profile of v5, /device:TPU:1, one launch (start us, length us, event | category | flops | bytes accessed | tf_op | source)
XLA Modules:
  0.0 59.0 jit_solution(17579500362193837743)
XLA Ops:
  0.0 0.7 %pad_add_fusion.1 = s32[25,64]{1,0:T(8,128)S(1)} fusion(s32[1,64]{1,0:T(1,128)} %param.7, s32[24,64]{1,0:T(8,128)} %bitcast.12), kind=kLoop, calls=%fused_computation.1 | loop fusion | flops 1600 | bytes 12800 | tf_op jit(solution)/shard_map/concatenate | solution.py:394
  0.7 0.7 %pad_add_fusion.small = s32[27,128]{1,0:T(8,128)S(1)} fusion(s32[25,64]{1,0:T(8,128)S(1)} %pad_add_fusion.1, s32[2,128]{1,0:T(2,128)} %bitcast.13), kind=kLoop, calls=%fused_computation | loop fusion | flops 3456 | bytes 21248 | tf_op jit(solution)/shard_map/concatenate | solution.py:395
  1.4 56.7 %shard_map.55 = f32[16,2,2,8,384]{4,3,2,1,0:T(8,128)S(1)} custom-call(bf16[64,96,128]{2,1,0:T(8,128)(2,1)} %bitcast.11, s32[27,128]{1,0:T(8,128)S(1)} %pad_add_fusion.small, bf16[3,6,256,128]{3,2,1,0:T(8,128)(2,1)} %constant.4.clone.tab), custom_call_target="tpu_custom_call" | custom-call | tf_op jit(solution)/shard_map/pallas_call | solution.py:400
  58.1 0.9 %copy.8 = f32[16,2,2,8,384]{4,3,2,1,0:T(8,128)} copy(f32[16,2,2,8,384]{4,3,2,1,0:T(8,128)S(1)} %shard_map.55) | data formatting | bytes 1572864
